TPU v7x, 32 devices: a whole 2x2x4 slice. The times are simulated.
32 devices in a mesh: src: 16 (over z, y, core), att: 2 (over x).
Axes of the slice: x: 2, y: 2, z: 4, core: 2. Of those that a mesh axis runs over, the one named last changes fastest.
Arguments:
- attitude: float32 [4, 512], P(None, 'att'), may hold values from -6 to 6
- obs_value: float32 [1048576], P(('src', 'att')), may hold values from -192 to 192
- obs_weight: float32 [1048576], P(('src', 'att')), may hold values from 0.5 to 5
- obs_time: float32 [1048576], P(('src', 'att')), may hold values from 0 to 1
- att_partials: float32 [4, 1048576], P(None, ('src', 'att')), may hold values from -6 to 6
- src_partials: float32 [5, 1048576], P(None, ('src', 'att')), may hold values from -6 to 6
- obs_source: int32 [1048576], P(('src', 'att')), may hold values from 0 to 4095
- knot_start: int32 [8192], P(('src', 'att')), may hold values from 0 to 508, as said below
- valid_count: int32 [8192], P(('src', 'att')), may hold values from 32 to 128
Outputs:
- attitude_step: float32 [4, 512], P(None, 'att')
- source_step: float32 [5, 65536], P(None, 'src')
Inputs may be any that keep to these rules, and one draw needn't show every extreme that they name: `obs_source`: index among the 4096 sources of the observation's src shard. `knot_start`: the blocks of a device at index a of att start in knots a * 256 to a * 256 + 256 - 1 (the segment that att index owns). `valid_count`: rows past the count are padding.
All inputs are finite; a program needn't handle non-finite values.
Results may differ from a plain program's by a relative error of at most 0.0003.
Values sent between devices are 32-bit elements; how exact they have to be, the bound alone decides.
A program may use at most 64 MiB of HBM per device.

v0:
```python
import jax
import jax.numpy as jnp
from jax import lax
from jax.sharding import PartitionSpec as P

ITERS = 4
SRC_DEV = 4096


OMEGA = 0.2
ATT_PRIOR = 1.0
SRC_PRIOR = 1.0
HIGH = lax.Precision.HIGHEST


def from_behind(value, axis, steps):
    count = lax.axis_size(axis)
    initial, last = (max(0, -steps), min(count, count - steps))
    return lax.ppermute(value, axis, [(source, source + steps) for source in range(initial, last)])


def extended(block, sides, width):
    for axis, dim in sides:
        count = lax.axis_size(axis)
        forward = [(i, i + 1) for i in range(count - 1)]
        backward = [(target, source) for source, target in forward]
        low = lax.ppermute(
            lax.slice_in_dim(block, block.shape[dim] - width, None, axis=dim), axis, forward
        )
        high = lax.ppermute(lax.slice_in_dim(block, 0, width, axis=dim), axis, backward)
        block = jnp.concatenate([low, block, high], axis=dim)
    return block


def spline_basis(phase):
    rest = 1.0 - phase
    square = phase * phase
    cube = square * phase
    return jnp.stack(
        [
            rest * rest * rest / 6.0,
            (3.0 * cube - 6.0 * square + 4.0) / 6.0,
            (-3.0 * cube + 3.0 * square + 3.0 * phase + 1.0) / 6.0,
            cube / 6.0,
        ]
    )


def pick_knots(attitude_full, knot_start):
    index = knot_start[:, None] + jnp.arange(4, dtype=jnp.int32)[None, :]
    return attitude_full[:, index]


def predict(att_blocks, basis, picked):
    return jnp.einsum("ibr,jbr,ibj->br", att_blocks, basis, picked, precision=HIGH)


def block_terms(att_blocks, basis, weight, resid):
    nblock = weight.shape[0]
    design = (att_blocks[:, None] * basis[None, :]).reshape(16, nblock, weight.shape[1])
    weighted = design * weight[None]
    gram = jnp.einsum("kbr,lbr->bkl", weighted, design, precision=HIGH)
    hvec = jnp.einsum("kbr,br->bk", weighted, resid, precision=HIGH)
    return (gram, hvec)


def block_rows(gram, hvec, knot_start):
    nblock = gram.shape[0]
    grams = gram.reshape(nblock, 4, 4, 4, 4)
    hparts = hvec.reshape(nblock, 4, 4)
    zeros = jnp.zeros((nblock, 4, 4), jnp.float32)
    row_sets = []
    for leading in range(4):
        pieces = []
        for distance in range(4):
            if leading + distance <= 3:
                pieces.append(grams[:, :, leading, :, leading + distance])
            else:
                pieces.append(zeros)
        banded = jnp.stack(pieces, axis=1).reshape(nblock, 64)
        row_sets.append(jnp.concatenate([banded, hparts[:, :, leading]], axis=1))
    stacked = jnp.stack(row_sets, axis=0).reshape(4 * nblock, 68)
    knot_ids = (knot_start[None, :] + jnp.arange(4, dtype=jnp.int32)[:, None]).reshape(4 * nblock)
    return (stacked, knot_ids)


def apply_band(band, band_ext, padded, count):
    image = jnp.zeros((4, count), jnp.float32)
    for distance in range(4):
        upper = padded[:, 3 + distance : 3 + distance + count]
        image = image + jnp.einsum("ijk,jk->ik", band[distance], upper, precision=HIGH)
        if distance > 0:
            lower_band = band_ext[distance][:, :, 3 - distance : 3 - distance + count]
            lower_step = padded[:, 3 - distance : 3 - distance + count]
            image = image + jnp.einsum("jik,jk->ik", lower_band, lower_step, precision=HIGH)
    return image


def solve_small(matrix, vector):
    entries = [[matrix[line, column] for column in range(5)] for line in range(5)]
    target = [vector[line] for line in range(5)]
    for pivot in range(5):
        for line in range(pivot + 1, 5):
            factor = entries[line][pivot] / entries[pivot][pivot]
            for column in range(pivot, 5):
                entries[line][column] = entries[line][column] - factor * entries[pivot][column]
            target[line] = target[line] - factor * target[pivot]
    result = [None] * 5
    for line in reversed(range(5)):
        total = target[line]
        for column in range(line + 1, 5):
            total = total - entries[line][column] * result[column]
        result[line] = total / entries[line][line]
    return jnp.stack(result)


def source_terms(partials, weight, resid):
    count = weight.shape[0]
    weighted = partials * weight[None, :]
    outer = (weighted[:, None, :] * partials[None, :, :]).reshape(25, count)
    right = weighted * resid[None, :]
    return jnp.concatenate([outer, right], axis=0).T


def finish_sources(sums):
    count = sums.shape[0]
    matrix = (
        sums[:, :25].T.reshape(5, 5, count) + SRC_PRIOR * jnp.eye(5, dtype=jnp.float32)[:, :, None]
    )
    return solve_small(matrix, sums[:, 25:].T)


def shards(
    attitude,
    obs_value,
    obs_weight,
    obs_time,
    att_partials,
    src_partials,
    obs_source,
    knot_start,
    valid_count,
):
    nblock = knot_start.shape[0]
    width = obs_value.shape[0] // nblock
    count = attitude.shape[1]
    first_knot = lax.axis_index("att") * count
    local_start = knot_start - first_knot
    following = from_behind(attitude[:, :3], "att", -1)
    attitude_local = jnp.concatenate([attitude, following], axis=1)
    basis = spline_basis(obs_time.reshape(nblock, width))
    position = jnp.arange(width, dtype=jnp.int32)[None, :]
    weight = jnp.where(position < valid_count[:, None], obs_weight.reshape(nblock, width), 0.0)
    att_blocks = att_partials.reshape(4, nblock, width)
    grid = obs_value.reshape(nblock, width)
    first_resid = grid - predict(att_blocks, basis, pick_knots(attitude_local, local_start))
    gram, hvec = block_terms(att_blocks, basis, weight, first_resid)
    rows, knot_ids = block_rows(gram, hvec, local_start)
    partial_value = jax.ops.segment_sum(rows, knot_ids, num_segments=count + 3)
    summed = lax.psum(partial_value, "src")
    incoming = from_behind(summed[count:], "att", 1)
    owned = jnp.concatenate([summed[:3] + incoming, summed[3:count]], axis=0)
    owned = owned.T
    band = owned[:64].reshape(4, 4, 4, count)
    rhs = owned[64:]
    band_prev = from_behind(band[:, :, :, count - 3 :], "att", 1)
    band_ext = jnp.concatenate([band_prev, band], axis=3)
    diagonal = band[0, jnp.arange(4), jnp.arange(4), :] + ATT_PRIOR

    def sweep(index, step):
        padded = extended(step, (("att", 1),), 3)
        image = apply_band(band, band_ext, padded, count) + ATT_PRIOR * step
        return step + OMEGA * (rhs - image) / diagonal

    step = lax.fori_loop(0, ITERS, sweep, jnp.zeros((4, count), jnp.float32))
    step_next = from_behind(step[:, :3], "att", -1)
    updated = attitude_local + jnp.concatenate([step, step_next], axis=1)
    second_resid = grid - predict(att_blocks, basis, pick_knots(updated, local_start))
    terms = source_terms(src_partials, weight.reshape(-1), second_resid.reshape(-1))
    sums = jax.ops.segment_sum(terms, obs_source, num_segments=SRC_DEV)
    source_step = finish_sources(lax.psum(sums, "att"))
    return (step, source_step)


def solution(mesh):
    in_specs = (
        P(None, "att"),
        P(("src", "att")),
        P(("src", "att")),
        P(("src", "att")),
        P(None, ("src", "att")),
        P(None, ("src", "att")),
        P(("src", "att")),
        P(("src", "att")),
        P(("src", "att")),
    )
    out_specs = (P(None, "att"), P(None, "src"))
    return jax.shard_map(shards, mesh=mesh, in_specs=in_specs, out_specs=out_specs, check_vma=False)
```

profile of v0, /device:TPU:0, one launch (start us, length us, event | category | flops | bytes accessed | tf_op | source)
XLA Modules:
  0.0 443.2 jit_solution(5113429531236415676)
XLA Ops:
  7.2 1.3 slice.226
  8.5 1.3 collective-permute-start.2
  12.6 1.0 fusion.43
  14.7 4.8 %fusion.26 = f32[256,16,16]{2,1,0:T(8,128)} fusion(f32[16,256,128]{2,0,1:T(8,128)S(1)} %bitcast.448, f32[256,128]{1,0:T(8,128)S(1)} %bitcast_select_fusion), kind=kOutput, calls=%fused_computation.54 | convolution fusion | flops 101187584 | bytes 2490368 | tf_op jit(solution)/shard_map/kbr,lbr->bkl/dot_general | solution.py:62
  19.5 3.2 copy.204
  22.7 1.7 reshape.1435
  24.4 1.9 slice_bitcast_fusion.39
  31.5 1.3 copy.302
  33.6 4.2 gather_fusion
  37.8 3.2 fusion.30
  41.0 4.0 fusion.24
  45.1 1.0 copy.276
  46.1 0.8 maximum_bitcast_fusion.2
  47.0 0.8 maximum_bitcast_fusion.3
  47.8 0.8 maximum_bitcast_fusion.4
  48.7 0.8 maximum_bitcast_fusion.5
  49.8 6.8 %scatter_custom_fusion = f32[259,68]{1,0:T(8,128)} fusion(s32[1024]{0:T(1024)} %bitcast.458, f32[1024,68]{1,0:T(8,128)S(1)} %bitcast.455, f32[]{:T(128)} %constant.18.clone.1), kind=kCustom, calls=%fused_computation.104 | custom fusion | flops 69632 | bytes 70960 | tf_op jit(solution)/shard_map/scatter-add | solution.py:159
  56.7 91.5 %all-reduce.3.cloned.1.call-done = f32[259,68]{1,0:T(8,128)} async-done(((f32[259,68]{1,0:T(8,128)}), f32[259,68]{1,0:T(8,128)}) %all-reduce.3.cloned.1.call-update) | async-done | bytes 70464 | tf_op jit(solution)/shard_map/psum | solution.py:160
  148.9 3.4 collective-permute-start.3
  152.3 0.9 slice.330
  154.4 4.2 collective-permute-start.4
  159.4 0.8 collective-permute-done.4
  160.3 32.9 %while.11 = (s32[]{:T(128)}, f32[4,256]{1,0:T(4,128)S(1)}, f32[4,4,4,256]{3,2,1,0:T(4,128)S(1)}, f32[4,4,4,259]{3,2,1,0:T(4,128)S(1)}, f32[4,256]{1,0:T(4,128)S(...) while((s32[]{:T(128)}, f32[4,256]{1,0:T(4,128)S(1)}, f32[4,4,4,256]{3,2,1,0:T(4,128)S(1)}, ...), condition=%wide.region_3.4_spmd.clone, body=%wide.region_2.3_spmd.clone.sunk | while | flops 70659 | bytes 362449 | solution.py:175
  160.4 4.2 collective-permute-start
  164.6 1.3 collective-permute-start.1
  166.0 4.1 collective-permute-done.1
  170.5 1.6 collective-permute-start
  172.2 1.3 collective-permute-start.1
  173.5 4.1 collective-permute-done.1
  178.1 1.6 collective-permute-start
  179.8 1.3 collective-permute-start.1
  181.1 4.1 collective-permute-done.1
  185.7 1.6 collective-permute-start
  187.3 1.3 collective-permute-start.1
  188.7 4.1 collective-permute-done.1
  193.2 1.3 collective-permute-start.5
  194.5 4.2 collective-permute-done.5
  198.8 3.0 gather_fusion.2
  201.9 2.2 fusion.31
  204.3 2.7 broadcast_multiply_fusion
  207.0 5.1 %mul.1017 = f32[25,32768]{1,0:T(8,128)} reshape(f32[5,5,32768]{2,1,0:T(8,128)} %broadcast_multiply_fusion) | data formatting | bytes 6553600 | tf_op jit(solution)/shard_map/mul | solution.py:120
  212.1 4.6 %maximum_bitcast_fusion = f32[32768,30]{0,1:T(8,128)} fusion(f32[5,32768]{1,0:T(8,128)S(1)} %get-tuple-element.125, f32[25,32768]{1,0:T(8,128)} %mul.1017), kind=kLoop, calls=%fused_computation.51 | loop fusion | flops 983040 | bytes 7864320 | tf_op jit(solution)/shard_map/transpose | solution.py:122
  216.7 10.4 %copy.225 = f32[32768,30]{1,0:T(8,128)} copy(f32[32768,30]{0,1:T(8,128)} %maximum_bitcast_fusion) | data formatting | bytes 7864320 | tf_op jit(solution)/shard_map/transpose | solution.py:122
  227.1 174.7 %scatter_custom_fusion.1 = f32[4096,30]{1,0:T(8,128)S(1)} fusion(s32[32768]{0:T(1024)} %param.17, f32[32768,30]{1,0:T(8,128)} %copy.225, f32[]{:T(128)} %constant.18.clone.1), kind=kCustom, calls=%fused_computation.63 | custom fusion | flops 983040 | bytes 492032 | tf_op jit(solution)/shard_map/scatter-add | solution.py:180
  401.8 1.4 copy.226
  403.3 29.3 %all-reduce.5.cloned.1.call-done = f32[4096,30]{0,1:T(8,128)} async-done(((f32[4096,30]{0,1:T(8,128)}), f32[4096,30]{0,1:T(8,128)}) %all-reduce.5.cloned.1.call-update) | async-done | bytes 491536 | tf_op jit(solution)/shard_map/psum | solution.py:181
  432.6 1.1 slice_bitcast_fusion.6
  434.1 0.9 slice_bitcast_fusion.7
  (121 shorter events, 16.9 us)
Async XLA Ops:
  7.2 6.8 %copy-start = (f32[4,32768]{1,0:T(4,128)S(1)}, f32[4,32768]{1,0:T(4,128)}, u32[]{:S(2)}) copy-start(f32[4,32768]{1,0:T(4,128)} %param.15) | copy-start | bytes 1572868
  7.2 141.0 %all-reduce.3.cloned.1.call-start = ((), (), s32[]{:S(2)}) async-start(), calls=%async_computation | async-start | bytes 270336 | tf_op jit(solution)/shard_map/psum | solution.py:160
  8.5 24.2 %collective-permute-start.2 = (f32[4,3]{1,0:T(4,128)}, f32[4,3]{1,0:T(4,128)}, u32[]{:S(2)}, u32[]{:S(2)}) collective-permute-start(f32[4,3]{1,0:T(4,128)} %slice.226), channel_id=1, source_target_pairs={{1,0},{3,2},{5,4},{7,6},{9,8},{11,10},{13,12},{15,14},{17,16},{19,... | collective-permute-start | bytes 152 | tf_op jit(solution)/shard_map/ppermute | solution.py:19
  13.6 0.9 copy-start.4
  13.6 0.9 copy-start.6
  33.6 7.4 %copy-start.3 = (f32[32768]{0:T(1024)S(1)}, f32[32768]{0:T(1024)}, u32[]{:S(2)}) copy-start(f32[32768]{0:T(1024)} %param.12) | copy-start | bytes 393220
  41.0 15.6 %copy-start.7 = (s32[256]{0:T(256)S(1)}, s32[256]{0:T(256)}, u32[]{:S(2)}) copy-start(s32[256]{0:T(256)} %param.19) | copy-start | bytes 3076
  45.1 11.5 %copy-start.5 = (f32[32768]{0:T(1024)S(1)}, f32[32768]{0:T(1024)}, u32[]{:S(2)}) copy-start(f32[32768]{0:T(1024)} %param.13) | copy-start | bytes 393220
  56.6 376.0 %all-reduce.5.cloned.1.call-start = ((), (), s32[]{:S(2)}) async-start(), calls=%async_computation.1 | async-start | bytes 1048576 | tf_op jit(solution)/shard_map/psum | solution.py:181
  148.9 4.7 %collective-permute-start.3 = (f32[3,68]{1,0:T(4,128)S(1)}, f32[3,68]{1,0:T(4,128)S(1)}, u32[]{:S(2)}, u32[]{:S(2)}) collective-permute-start(f32[3,68]{1,0:T(4,128)S(1)} %slice.329), channel_id=1, source_target_pairs={{0,1},{2,3},{4,5},{6,7},{8,9},{10,11},{12,13},{14,15},{16,17},{18,... | collective-permute-start | bytes 2456 | tf_op jit(solution)/shard_map/ppermute | solution.py:19
  154.4 5.8 %collective-permute-start.4 = (f32[4,4,4,3]{3,2,1,0:T(4,128)S(1)}, f32[4,4,4,3]{3,2,1,0:T(4,128)S(1)}, u32[]{:S(2)}, u32[]{:S(2)}) collective-permute-start(f32[4,4,4,3]{3,2,1,0:T(4,128)S(1)} %slice.332), channel_id=1, source_target_pairs={{0,1},{2,3},{4,5},{6,7},{8,9},{10,11},{12,13},{14,15},{16,17},{18,... | collective-permute-start | bytes 2312 | tf_op jit(solution)/shard_map/ppermute | solution.py:19
  160.4 5.6 %collective-permute-start = (f32[4,3]{1,0:T(4,128)S(1)}, f32[4,3]{1,0:T(4,128)S(1)}, u32[]{:S(2)}, u32[]{:S(2)}) collective-permute-start(f32[4,3]{1,0:T(4,128)S(1)} %get-tuple-element.231), channel_id=1, source_target_pairs={{0,1},{2,3},{4,5},{6,7},{8,9},{10,11},{12,13},{14,15},{16,17},{18,... | collective-permute-start | bytes 152 | tf_op jit(solution)/shard_map/while/body/eval_jaxpr/ppermute | solution.py:27
  164.6 5.5 %collective-permute-start.1 = (f32[4,3]{1,0:T(4,128)S(1)}, f32[4,3]{1,0:T(4,128)S(1)}, u32[]{:S(2)}, u32[]{:S(2)}) collective-permute-start(f32[4,3]{1,0:T(4,128)S(1)} %get-tuple-element.232), channel_id=1, source_target_pairs={{1,0},{3,2},{5,4},{7,6},{9,8},{11,10},{13,12},{15,14},{17,16},{19,... | collective-permute-start | bytes 152 | tf_op jit(solution)/shard_map/while/body/eval_jaxpr/ppermute | solution.py:30
  170.5 3.0 collective-permute-start
  172.2 5.5 %collective-permute-start.1 = (f32[4,3]{1,0:T(4,128)S(1)}, f32[4,3]{1,0:T(4,128)S(1)}, u32[]{:S(2)}, u32[]{:S(2)}) collective-permute-start(f32[4,3]{1,0:T(4,128)S(1)} %get-tuple-element.232), channel_id=1, source_target_pairs={{1,0},{3,2},{5,4},{7,6},{9,8},{11,10},{13,12},{15,14},{17,16},{19,... | collective-permute-start | bytes 152 | tf_op jit(solution)/shard_map/while/body/eval_jaxpr/ppermute | solution.py:30
  178.1 3.0 collective-permute-start
  179.8 5.5 %collective-permute-start.1 = (f32[4,3]{1,0:T(4,128)S(1)}, f32[4,3]{1,0:T(4,128)S(1)}, u32[]{:S(2)}, u32[]{:S(2)}) collective-permute-start(f32[4,3]{1,0:T(4,128)S(1)} %get-tuple-element.232), channel_id=1, source_target_pairs={{1,0},{3,2},{5,4},{7,6},{9,8},{11,10},{13,12},{15,14},{17,16},{19,... | collective-permute-start | bytes 152 | tf_op jit(solution)/shard_map/while/body/eval_jaxpr/ppermute | solution.py:30
  185.7 3.0 collective-permute-start
  187.3 5.5 %collective-permute-start.1 = (f32[4,3]{1,0:T(4,128)S(1)}, f32[4,3]{1,0:T(4,128)S(1)}, u32[]{:S(2)}, u32[]{:S(2)}) collective-permute-start(f32[4,3]{1,0:T(4,128)S(1)} %get-tuple-element.232), channel_id=1, source_target_pairs={{1,0},{3,2},{5,4},{7,6},{9,8},{11,10},{13,12},{15,14},{17,16},{19,... | collective-permute-start | bytes 152 | tf_op jit(solution)/shard_map/while/body/eval_jaxpr/ppermute | solution.py:30
  193.2 8.7 %copy-start.2 = (f32[4,256]{1,0:T(4,128)}, f32[4,256]{1,0:T(4,128)S(1)}, u32[]{:S(2)}) copy-start(f32[4,256]{1,0:T(4,128)S(1)} %get-tuple-element.72) | copy-start | bytes 12292
  193.2 5.5 %collective-permute-start.5 = (f32[4,3]{1,0:T(4,128)S(1)}, f32[4,3]{1,0:T(4,128)S(1)}, u32[]{:S(2)}, u32[]{:S(2)}) collective-permute-start(f32[4,3]{1,0:T(4,128)S(1)} %slice.243), channel_id=1, source_target_pairs={{1,0},{3,2},{5,4},{7,6},{9,8},{11,10},{13,12},{15,14},{17,16},{19,... | collective-permute-start | bytes 152 | tf_op jit(solution)/shard_map/ppermute | solution.py:19
  201.9 2.2 copy-start.1
Sparse Core Ops, SparseCore 0:
  56.7 91.4 all-reduce.2
  403.4 29.1 all-reduce.4
where the time goes:
time: 445 us; the launch traced here: 443 us
  other arithmetic  199 us (45%)
  waiting for transfers between devices  143 us (32%)
  local copies, waits for them, and re-layouts  47.6 us (11%)
  starting transfers between devices  24.5 us (6%)
  between operations  14.5 us (3%)
  matrix products  14.2 us (3%)
    scatter-add x1, other arithmetic, shards(): sums = jax.ops.segment_sum(terms, obs_source, num_segments=SRC_DEV)  175 us
    psum x1, waiting for transfers between devices, shards(): summed = lax.psum(partial_value, 'src')  91.5 us
    psum x1, waiting for transfers between devices, shards(): source_step = finish_sources(lax.psum(sums, 'att'))  29.3 us
    ppermute x4, waiting for transfers between devices, extended(): lax.ppermute(lax.slice_in_dim(block, 0, width, axis=dim), axis, backward)  16.6 us
    transpose x1, local copies, waits for them, and re-layouts, source_terms(): return jnp.concatenate([outer, right], axis=0).T  10.4 us
    ppermute x4, starting transfers between devices, from_behind(): lax.ppermute(value, axis, [(source, source + steps) for source in range(i...  10.1 us
    ppermute x4, starting transfers between devices, extended(): lax.ppermute(lax.slice_in_dim(block, block.shape[dim] - width, None, axis...  9.14 us
  transfers between devices with their start and end apart: 14, of which 9 were waited for; matrix products, arithmetic and copies ran while one was open for 6% of the time, Pallas kernels for 0%

commit v1 on v0

v1 whole, which is shorter than its diff:
```python
import functools

import jax
import jax.numpy as jnp
from jax import lax
from jax.experimental import pallas as pl
from jax.experimental.pallas import tpu as pltpu
from jax.sharding import PartitionSpec as P

ITERS = 4
SRC_DEV = 4096
OMEGA = 0.2
ATT_PRIOR = 1.0
SRC_PRIOR = 1.0
HIGH = lax.Precision.HIGHEST
MESH = pl.DeviceIdType.MESH

PAIRS = [(i, j) for i in range(4) for j in range(i, 4)]
PAIR_AT = {}
for _n, (_i, _j) in enumerate(PAIRS):
    PAIR_AT[(_i, _j)] = _n
    PAIR_AT[(_j, _i)] = _n
BAND_ROWS = 48
USED_ROWS = 44
STEP = 512
HI = 256
LO = SRC_DEV // HI


def basis_of(u):
    rest = 1.0 - u
    square = u * u
    cube = square * u
    return [
        rest * rest * rest / 6.0,
        (3.0 * cube - 6.0 * square + 4.0) / 6.0,
        (-3.0 * cube + 3.0 * square + 3.0 * u + 1.0) / 6.0,
        cube / 6.0,
    ]


def dot_last(a, b, precision=None):
    return lax.dot_general(
        a, b, (((1,), (1,)), ((), ())), precision=precision, preferred_element_type=jnp.float32
    )


def kernel(
    n_src,
    n_att,
    att_ref,
    val_ref,
    wgt_ref,
    time_ref,
    apart_ref,
    spart_ref,
    ids_ref,
    knot_ref,
    valid_ref,
    step_ref,
    out_ref,
    vt,
    pt,
    bt,
    wr,
    rr,
    wpp,
    zrows,
    part,
    slots,
    full,
    left,
    right,
    att_left,
    att_right,
    acc_s,
    acc_g,
    s_slots,
    g_slots,
    rs_send,
    rs_recv,
    ag_send,
    ag_recv,
    l_send,
    l_recv,
    r_send,
    r_recv,
    a_send,
    a_recv,
    s_send,
    s_recv,
    g_send,
    g_recv,
):
    me = lax.axis_index("src")
    seg = lax.axis_index("att")
    per = part.shape[1]
    nblock, width = val_ref.shape
    count = att_ref.shape[1]
    barrier = pltpu.get_barrier_semaphore()

    def greet(t, carry):
        pl.semaphore_signal(
            barrier,
            inc=1,
            device_id=(lax.rem(me + t, n_src), seg),
            device_id_type=MESH,
        )
        return carry

    lax.fori_loop(1, n_src, greet, 0)
    for t in range(1, n_att):

        def greet_across(s, carry, t=t):
            pl.semaphore_signal(
                barrier, inc=1, device_id=(s, lax.rem(seg + t, n_att)), device_id_type=MESH
            )
            return carry

        lax.fori_loop(0, n_src, greet_across, 0)

    position = lax.broadcasted_iota(jnp.int32, (width, nblock), 0)
    weight = jnp.where(position < valid_ref[...], wgt_ref[...].T, 0.0)
    wr[...] = weight.T
    vt[0] = weight
    value = val_ref[...].T
    vt[1] = value
    basis = basis_of(time_ref[...].T)
    for j in range(4):
        bt[j] = basis[j]
        pt[j] = apart_ref[j].T
    wvalue = weight * value
    for n, (i, j) in enumerate(PAIRS):
        wpp[n] = weight * pt[i] * pt[j]
    for i in range(4):
        wpp[10 + i] = wvalue * pt[i]
    zrows[...] = jnp.zeros_like(zrows)
    for j0 in range(4):
        for d in range(4 - j0):
            both = bt[j0] * bt[j0 + d]
            for n in range(10):
                row = j0 * BAND_ROWS + d * 10 + n
                zrows[row : row + 1, :] = jnp.sum(wpp[n] * both, axis=0, keepdims=True)
        for i in range(4):
            row = j0 * BAND_ROWS + 40 + i
            zrows[row : row + 1, :] = jnp.sum(wpp[10 + i] * bt[j0], axis=0, keepdims=True)
    local = knot_ref[...] - seg * count
    knots = lax.broadcasted_iota(jnp.int32, (count, nblock), 0)
    hot = jnp.where(knots == local, 1.0, 0.0)
    placed = dot_last(zrows[...], hot, HIGH)
    placed = jnp.concatenate(
        [placed, jnp.zeros((4 * BAND_ROWS, 128), jnp.float32)], axis=1
    )
    rows = placed[:BAND_ROWS]
    for j0 in range(1, 4):
        rows = rows + pltpu.roll(placed[j0 * BAND_ROWS : (j0 + 1) * BAND_ROWS], j0, 1)
    for c in range(n_src):
        top = min((c + 1) * per, BAND_ROWS)
        if c * per < BAND_ROWS:
            if top - c * per == per:
                part[c] = rows[c * per : top]
            else:
                part[c] = jnp.zeros(part.shape[1:], jnp.float32)
                part[c, : top - c * per] = rows[c * per : top]
        else:
            part[c] = jnp.zeros(part.shape[1:], jnp.float32)

    pl.semaphore_wait(barrier, n_src * n_att - 1)

    def rs_copy(t):
        c = lax.rem(me + t, n_src)
        return pltpu.make_async_remote_copy(
            src_ref=part.at[c],
            dst_ref=slots.at[me],
            send_sem=rs_send.at[c],
            recv_sem=rs_recv.at[me],
            device_id=(c, seg),
            device_id_type=MESH,
        )

    def rs_wait(t):
        s = lax.rem(me + t, n_src)
        return pltpu.make_async_remote_copy(
            src_ref=part.at[s],
            dst_ref=slots.at[s],
            send_sem=rs_send.at[s],
            recv_sem=rs_recv.at[s],
            device_id=(s, seg),
            device_id_type=MESH,
        )

    def att_copy(dst, slot, shift):
        return pltpu.make_async_remote_copy(
            src_ref=att_ref,
            dst_ref=dst,
            send_sem=a_send.at[slot],
            recv_sem=a_recv.at[slot],
            device_id=(me, lax.rem(seg + shift + n_att, n_att)),
            device_id_type=MESH,
        )

    def run(make):
        def body(t, carry):
            make(t).start()
            return carry

        return body

    def finish(make):
        def body(t, carry):
            make(t).wait()
            return carry

        return body

    slots[me] = part[me]
    lax.fori_loop(1, n_src, run(rs_copy), 0)
    to_right = att_copy(att_left, 0, 1)
    to_left = att_copy(att_right, 1, -1)
    to_right.start()
    to_left.start()

    lanes = lax.broadcasted_iota(jnp.int32, (HI, 1), 0).astype(jnp.float32)
    blocks = STEP // width

    def row_of(ref, g):
        return jnp.concatenate(
            [ref[pl.ds(g * blocks + t, 1), :] for t in range(blocks)], axis=1
        )

    def hot_pair(g):
        ids = row_of(ids_ref, g)
        low = jnp.bitwise_and(ids, HI - 1).astype(jnp.float32).astype(jnp.bfloat16)
        high = jnp.right_shift(ids, 8).astype(jnp.float32).astype(jnp.bfloat16)
        base = jnp.broadcast_to(low, (HI, STEP))
        lane_hot = jnp.where(
            base == jnp.broadcast_to(lanes.astype(jnp.bfloat16), (HI, STEP)),
            jnp.bfloat16(1),
            jnp.bfloat16(0),
        )
        return lane_hot, jnp.broadcast_to(high, (16, STEP))

    def spread(terms, high):
        parts = []
        zero = jnp.zeros((16, STEP), jnp.bfloat16)
        for line in range(LO):
            mask = high == jnp.bfloat16(line)
            for term in terms:
                parts.append(jnp.where(mask, term, zero))
        return jnp.concatenate(parts, axis=0)

    def s_step(g, carry):
        lane_hot, high = hot_pair(g)
        p = spart_ref[:, pl.ds(pl.multiple_of(g * STEP, STEP), STEP)]
        wp = p * row_of(wr, g)
        p1 = jnp.concatenate([p[1:], p[:1]], axis=0)
        p2 = jnp.concatenate([p[2:], p[:2]], axis=0)
        terms = jnp.concatenate(
            [wp * p, wp * p1, wp * p2, jnp.zeros((1, STEP), jnp.float32)], axis=0
        )
        coarse = terms.astype(jnp.bfloat16)
        fine = (terms - coarse.astype(jnp.float32)).astype(jnp.bfloat16)
        got = dot_last(spread([coarse, fine], high), lane_hot)
        acc_s[0] += got[:, :128]
        acc_s[1] += got[:, 128:]
        return carry

    steps = nblock * width // STEP
    acc_s[...] = jnp.zeros_like(acc_s)
    lax.fori_loop(0, steps // 2, s_step, 0)

    lax.fori_loop(1, n_src, finish(rs_wait), 0)
    total = slots[0]
    for s in range(1, n_src):
        total = total + slots[s]
    full[me] = total

    def ag_copy(t):
        c = lax.rem(me + t, n_src)
        return pltpu.make_async_remote_copy(
            src_ref=full.at[me],
            dst_ref=full.at[me],
            send_sem=ag_send.at[c],
            recv_sem=ag_recv.at[me],
            device_id=(c, seg),
            device_id_type=MESH,
        )

    def ag_wait(t):
        s = lax.rem(me + t, n_src)
        return pltpu.make_async_remote_copy(
            src_ref=full.at[s],
            dst_ref=full.at[s],
            send_sem=ag_send.at[s],
            recv_sem=ag_recv.at[s],
            device_id=(s, seg),
            device_id_type=MESH,
        )

    def right_copy(c, slot):
        return pltpu.make_async_remote_copy(
            src_ref=full.at[slot, :, pl.ds(count - 128, 256)],
            dst_ref=left.at[slot],
            send_sem=r_send.at[c],
            recv_sem=r_recv.at[slot],
            device_id=(c, lax.rem(seg + 1, n_att)),
            device_id_type=MESH,
        )

    def left_copy(c, slot):
        return pltpu.make_async_remote_copy(
            src_ref=full.at[slot, :, pl.ds(0, 128)],
            dst_ref=right.at[slot],
            send_sem=l_send.at[c],
            recv_sem=l_recv.at[slot],
            device_id=(c, lax.rem(seg + n_att - 1, n_att)),
            device_id_type=MESH,
        )

    lax.fori_loop(1, n_src, run(ag_copy), 0)

    @pl.when(seg < n_att - 1)
    def _():
        lax.fori_loop(0, n_src, run(lambda t: right_copy(lax.rem(me + t, n_src), me)), 0)

    @pl.when(seg > 0)
    def _():
        lax.fori_loop(0, n_src, run(lambda t: left_copy(lax.rem(me + t, n_src), me)), 0)

    lax.fori_loop(steps // 2, steps, s_step, 0)

    def mine(buf, c, half):
        return buf[c, :, half * 128 : half * 128 + 128]

    for c in range(15):
        for half in range(2):
            s_slots[seg, c, :, half * 128 : half * 128 + 128] = (
                acc_s[half, pl.ds(c, LO, stride=32), :]
                + acc_s[half, pl.ds(16 + c, LO, stride=32), :]
            )

    def across(buf, send, recv, t, slot):
        return pltpu.make_async_remote_copy(
            src_ref=buf.at[slot],
            dst_ref=buf.at[slot],
            send_sem=send.at[t],
            recv_sem=recv.at[slot],
            device_id=(me, lax.rem(seg + t, n_att)),
            device_id_type=MESH,
        )

    for t in range(1, n_att):
        across(s_slots, s_send, s_recv, t, seg).start()

    lax.fori_loop(1, n_src, finish(ag_wait), 0)

    @pl.when(seg < n_att - 1)
    def _():
        def body(t, carry):
            right_copy(t, me).wait_send()
            left_copy(t, t).wait_recv()
            return carry

        lax.fori_loop(0, n_src, body, 0)

    @pl.when(seg > 0)
    def _():
        def body(t, carry):
            left_copy(t, me).wait_send()
            right_copy(t, t).wait_recv()
            return carry

        lax.fori_loop(0, n_src, body, 0)

    @pl.when(seg == 0)
    def _():
        left[...] = jnp.zeros_like(left)

    @pl.when(seg == n_att - 1)
    def _():
        right[...] = jnp.zeros_like(right)

    to_right.wait()
    to_left.wait()

    def wide(row):
        c, t = divmod(row, per)
        own = full[c, t : t + 1, :]
        before = left[c, t : t + 1, :]
        after = right[c, t : t + 1, :]
        return jnp.concatenate(
            [
                before[:, :128],
                own[:, :128] + before[:, 128:],
                own[:, 128:count],
                own[:, count:] + after,
            ],
            axis=1,
        )

    line = [wide(row) for row in range(USED_ROWS)]
    band = [
        [
            jnp.concatenate([line[d * 10 + PAIR_AT[(i, j)]] for i in range(4)], axis=0)
            for j in range(4)
        ]
        for d in range(4)
    ]
    right_side = jnp.concatenate(line[40:44], axis=0)
    diagonal = (
        jnp.concatenate([line[PAIR_AT[(i, i)]] for i in range(4)], axis=0) + ATT_PRIOR
    )
    span = count + 256
    zero_halo = jnp.zeros((4, 128), jnp.float32)
    coeff = jnp.concatenate(
        [
            jnp.where(seg > 0, att_left[:, count - 128 :], zero_halo),
            att_ref[...],
            jnp.where(seg < n_att - 1, att_right[:, :128], zero_halo),
        ],
        axis=1,
    )

    def apply(vec):
        image = jnp.zeros_like(vec)
        for d in range(4):
            ahead = vec if d == 0 else pltpu.roll(vec, span - d, 1)
            low = jnp.zeros_like(vec)
            for j in range(4):
                image = image + band[d][j] * ahead[j : j + 1]
                if d > 0:
                    low = low + band[d][j] * vec[j : j + 1]
            if d > 0:
                image = image + pltpu.roll(low, d, 1)
        return image

    right_side = right_side - apply(coeff)
    step = OMEGA * right_side / diagonal
    for _ in range(ITERS - 1):
        step = step + OMEGA * (right_side - apply(step) - ATT_PRIOR * step) / diagonal
    step_ref[...] = step[:, 128 : 128 + count]
    updated = coeff + step
    shifted = jnp.concatenate(
        [
            (updated if j == 0 else pltpu.roll(updated, span - j, 1))[:, 128 : 128 + count]
            for j in range(4)
        ],
        axis=0,
    )
    hot2 = jnp.where(
        lax.broadcasted_iota(jnp.int32, (count, nblock), 0) == knot_ref[...] - seg * count, 1.0, 0.0
    )
    picked = lax.dot_general(
        shifted,
        hot2,
        (((1,), (0,)), ((), ())),
        precision=HIGH,
        preferred_element_type=jnp.float32,
    )
    resid = vt[1]
    for i in range(4):
        knot_sum = jnp.zeros((width, nblock), jnp.float32)
        for j in range(4):
            knot_sum = knot_sum + bt[j] * picked[j * 4 + i : j * 4 + i + 1]
        resid = resid - pt[i] * knot_sum
    rr[...] = (vt[0] * resid).T

    def g_step(g, carry):
        lane_hot, high = hot_pair(g)
        p = spart_ref[:, pl.ds(pl.multiple_of(g * STEP, STEP), STEP)]
        terms = jnp.concatenate(
            [p * row_of(rr, g), jnp.zeros((3, STEP), jnp.float32)], axis=0
        )
        coarse = terms.astype(jnp.bfloat16).astype(jnp.float32)
        both = jnp.concatenate([coarse, terms - coarse], axis=0).astype(jnp.bfloat16)
        got = dot_last(spread([both], high), lane_hot)
        acc_g[0] += got[:, :128]
        acc_g[1] += got[:, 128:]
        return carry

    acc_g[...] = jnp.zeros_like(acc_g)
    lax.fori_loop(0, steps, g_step, 0)
    for c in range(5):
        for half in range(2):
            g_slots[seg, c, :, half * 128 : half * 128 + 128] = (
                acc_g[half, pl.ds(c, LO, stride=16), :]
                + acc_g[half, pl.ds(8 + c, LO, stride=16), :]
            )
    for t in range(1, n_att):
        across(g_slots, g_send, g_recv, t, seg).start()

    def collect(buf, send, recv):
        for t in range(1, n_att):
            across(buf, send, recv, t, seg).wait_send()
            across(buf, send, recv, t, lax.rem(seg + t, n_att)).wait_recv()

    collect(s_slots, s_send, s_recv)

    def summed(buf, c):
        got = buf[0, c]
        for a in range(1, n_att):
            got = got + buf[a, c]
        return got

    entries = [[None] * 5 for _ in range(5)]
    for k in range(3):
        for i in range(5):
            got = summed(s_slots, k * 5 + i)
            other = (i + k) % 5
            if k == 0:
                got = got + SRC_PRIOR
            entries[i][other] = got
            entries[other][i] = got
    factors = {}
    for pivot in range(5):
        for row in range(pivot + 1, 5):
            factor = entries[row][pivot] / entries[pivot][pivot]
            factors[(row, pivot)] = factor
            for column in range(pivot + 1, 5):
                entries[row][column] = entries[row][column] - factor * entries[pivot][column]

    collect(g_slots, g_send, g_recv)
    target = [summed(g_slots, c) for c in range(5)]
    for pivot in range(5):
        for row in range(pivot + 1, 5):
            target[row] = target[row] - factors[(row, pivot)] * target[pivot]
    result = [None] * 5
    for row in reversed(range(5)):
        got = target[row]
        for column in range(row + 1, 5):
            got = got - entries[row][column] * result[column]
        result[row] = got / entries[row][row]
    for c in range(5):
        for a in range(LO):
            out_ref[c : c + 1, a * HI : (a + 1) * HI] = result[c][a : a + 1, :]


def solution(mesh):
    n_src = mesh.shape["src"]
    n_att = mesh.shape["att"]

    def shards(
        attitude,
        obs_value,
        obs_weight,
        obs_time,
        att_partials,
        src_partials,
        obs_source,
        knot_start,
        valid_count,
    ):
        nblock = knot_start.shape[0]
        width = obs_value.shape[0] // nblock
        count = attitude.shape[1]
        per = -(-USED_ROWS // n_src)
        f32 = jnp.float32
        dma = pltpu.SemaphoreType.DMA
        vmem = pl.BlockSpec(memory_space=pltpu.VMEM)
        tall = (width, nblock)
        return pl.pallas_call(
            functools.partial(kernel, n_src, n_att),
            out_shape=(
                jax.ShapeDtypeStruct((4, count), f32),
                jax.ShapeDtypeStruct((5, SRC_DEV), f32),
            ),
            in_specs=[vmem] * 9,
            out_specs=(vmem, vmem),
            scratch_shapes=[
                pltpu.VMEM((2,) + tall, f32),
                pltpu.VMEM((4,) + tall, f32),
                pltpu.VMEM((4,) + tall, f32),
                pltpu.VMEM((nblock, width), f32),
                pltpu.VMEM((nblock, width), f32),
                pltpu.VMEM((14,) + tall, f32),
                pltpu.VMEM((4 * BAND_ROWS, nblock), f32),
                pltpu.VMEM((n_src, per, count + 128), f32),
                pltpu.VMEM((n_src, per, count + 128), f32),
                pltpu.VMEM((n_src, per, count + 128), f32),
                pltpu.VMEM((n_src, per, 256), f32),
                pltpu.VMEM((n_src, per, 128), f32),
                pltpu.VMEM((4, count), f32),
                pltpu.VMEM((4, count), f32),
                pltpu.VMEM((2, LO * 32, 128), f32),
                pltpu.VMEM((2, LO * 16, 128), f32),
                pltpu.VMEM((n_att, 15, LO, HI), f32),
                pltpu.VMEM((n_att, 5, LO, HI), f32),
                dma((n_src,)),
                dma((n_src,)),
                dma((n_src,)),
                dma((n_src,)),
                dma((n_src,)),
                dma((n_src,)),
                dma((n_src,)),
                dma((n_src,)),
                dma((2,)),
                dma((2,)),
                dma((n_att,)),
                dma((n_att,)),
                dma((n_att,)),
                dma((n_att,)),
            ],
            compiler_params=pltpu.CompilerParams(
                collective_id=0,
                has_side_effects=True,
                vmem_limit_bytes=48 * 1024 * 1024,
            ),
        )(
            attitude,
            obs_value.reshape(nblock, width),
            obs_weight.reshape(nblock, width),
            obs_time.reshape(nblock, width),
            att_partials.reshape(4, nblock, width),
            src_partials,
            obs_source.reshape(nblock, width),
            knot_start.reshape(1, nblock),
            valid_count.reshape(1, nblock),
        )

    in_specs = (
        P(None, "att"),
        P(("src", "att")),
        P(("src", "att")),
        P(("src", "att")),
        P(None, ("src", "att")),
        P(None, ("src", "att")),
        P(("src", "att")),
        P(("src", "att")),
        P(("src", "att")),
    )
    out_specs = (P(None, "att"), P(None, "src"))
    return jax.shard_map(shards, mesh=mesh, in_specs=in_specs, out_specs=out_specs, check_vma=False)
```

time: 445 us -> 60.9 us (0.14)
  other arithmetic: 199 us -> 0 us
  waiting for transfers between devices: 143 us -> 0 us
  Pallas kernels: 0 us -> 53.2 us
  local copies, waits for them, and re-layouts: 47.6 us -> 6.75 us
  starting transfers between devices: 24.5 us -> 0 us
  matrix products: 14.2 us -> 0 us
  between operations: 14.5 us -> 0.68 us
    scatter-add x2 -> x0, other arithmetic: 181 us -> none  [the longest x1 175 us: shards(): sums = jax.ops.segment_sum(terms, obs_source, num_segments=SRC_DEV)]
    psum x2 -> x0, waiting for transfers between devices: 121 us -> none  [the longest x1 91.5 us: shards(): summed = lax.psum(partial_value, 'src')]
    pallas_call x0 -> x1, Pallas kernels: none -> 53.2 us  [shards(): pl.pallas_call(functools.partial(kernel, n_src, n_att), out_shape=(jax.Sh...]
    ppermute x12 -> x0, starting transfers between devices: 24.4 us -> none  [the longest x4 10.1 us: from_behind(): lax.ppermute(value, axis, [(source, source + steps) for source in range(i...]
    ppermute x12 -> x0, waiting for transfers between devices: 21.9 us -> none  [the longest x4 16.6 us: extended(): lax.ppermute(lax.slice_in_dim(block, 0, width, axis=dim), axis, backward)]
    dot_general x4 -> x0, matrix products: 14.2 us -> none  [the longest x2 5.38 us: predict(): jnp.einsum('ibr,jbr,ibj->br', att_blocks, basis, picked, precision=HIGH)]
    transpose x3 -> x0, local copies, waits for them, and re-layouts: 12.4 us -> none  [the longest x1 10.4 us: source_terms(): return jnp.concatenate([outer, right], axis=0).T]
    gather x3 -> x0, local copies, waits for them, and re-layouts: 7.82 us -> none  [the longest x2 7.22 us: pick_knots(): return attitude_full[:, index]]
  transfers between devices with their start and end apart: 14 -> 0, of which waited for: 9 -> 0; matrix products, arithmetic and copies ran while one was open for 6% -> 0% of each run, Pallas kernels for 0% -> 0%
where the time goes in v1:
time: 60.9 us; the launch traced here: 60.7 us
  Pallas kernels  53.2 us (87%)
  local copies, waits for them, and re-layouts  6.75 us (11%)
  between operations  0.68 us (1%)
    pallas_call x1, Pallas kernels, shards(): pl.pallas_call(functools.partial(kernel, n_src, n_att), out_shape=(jax.Sh...  53.2 us
    unnamed x19, local copies, waits for them, and re-layouts  6.75 us

profile of v1, /device:TPU:0, one launch (start us, length us, event | category | flops | bytes accessed | tf_op | source)
XLA Modules:
  0.0 60.7 jit_solution(17770655451691765809)
XLA Ops:
  0.6 0.0 copy-start
  0.6 0.0 copy-start.5
  0.7 0.0 copy-start.7
  0.7 1.2 %copy.13 = f32[1,4,256,128]{3,2,1,0:T(8,128)S(1)} copy(f32[1,4,256,128]{3,1,2,0:T(4,128)} %bitcast.17) | data formatting | bytes 1048576
  1.8 0.0 copy-start.6
  1.8 0.2 copy-done
  2.0 0.0 copy-done.5
  2.0 0.0 copy-done.7
  2.0 0.5 copy-done.6
  2.6 0.0 copy-start.1
  2.6 0.9 %copy-done.1 = f32[32768]{0:T(1024)S(1)} copy-done((f32[32768]{0:T(1024)S(1)}, f32[32768]{0:T(1024)}, u32[]{:S(2)}) %copy-start.1) | copy-done | bytes 131096
  3.5 0.0 copy-start.2
  3.5 0.9 %copy-done.2 = f32[32768]{0:T(1024)S(1)} copy-done((f32[32768]{0:T(1024)S(1)}, f32[32768]{0:T(1024)}, u32[]{:S(2)}) %copy-start.2) | copy-done | bytes 131096
  4.4 0.0 copy-start.3
  4.4 0.9 %copy-done.3 = f32[32768]{0:T(1024)S(1)} copy-done((f32[32768]{0:T(1024)S(1)}, f32[32768]{0:T(1024)}, u32[]{:S(2)}) %copy-start.3) | copy-done | bytes 131096
  5.3 0.0 copy-start.4
  5.3 0.9 %copy-done.4 = s32[32768]{0:T(1024)S(1)} copy-done((s32[32768]{0:T(1024)S(1)}, s32[32768]{0:T(1024)}, u32[]{:S(2)}) %copy-start.4) | copy-done | bytes 131096
  6.2 53.2 %shard_map.104 = (f32[4,256]{1,0:T(4,128)S(1)}, f32[5,4096]{1,0:T(8,128)S(1)}) custom-call(f32[4,256]{1,0:T(4,128)S(1)} %copy-done.5, f32[256,128]{1,0:T(8,128)S(1)} %bitcast.11, f32[256,128]{1,0:T(8,128)S(1)} %bitcast.12, f32[256,128]{1,0:T(8,128)S(1)} %bitcast.13, f32[4,256,128]{2,1,0:T(8,128)S(1)} %bitcast.10, f32[5,32768]{1,0:T(8,128)S(1)} %copy-done, ...), custom_call_target="tpu_custom_call" | custom-call | tf_op jit(solution)/shard_map/pallas_call | solution.py:561
  59.4 0.6 copy.16
  60.0 0.7 %copy.17 = f32[5,4096]{1,0:T(8,128)} copy(f32[5,4096]{1,0:T(8,128)S(1)} %get-tuple-element.5) | data formatting | bytes 163840
Async XLA Ops:
  0.6 1.4 %copy-start = (f32[5,32768]{1,0:T(8,128)S(1)}, f32[5,32768]{1,0:T(8,128)}, u32[]{:S(2)}) copy-start(f32[5,32768]{1,0:T(8,128)} %spart_ref.1) | copy-start | bytes 1966084
  0.6 1.4 %copy-start.5 = (f32[4,256]{1,0:T(4,128)S(1)}, f32[4,256]{1,0:T(4,128)}, u32[]{:S(2)}) copy-start(f32[4,256]{1,0:T(4,128)} %att_ref.1) | copy-start | bytes 12292
  0.7 1.4 %copy-start.7 = (s32[256]{0:T(256)S(1)}, s32[256]{0:T(256)}, u32[]{:S(2)}) copy-start(s32[256]{0:T(256)} %param.17) | copy-start | bytes 3076
  1.8 0.7 %copy-start.6 = (s32[256]{0:T(256)S(1)}, s32[256]{0:T(256)}, u32[]{:S(2)}) copy-start(s32[256]{0:T(256)} %param.16) | copy-start | bytes 3076
  2.6 0.9 %copy-start.1 = (f32[32768]{0:T(1024)S(1)}, f32[32768]{0:T(1024)}, u32[]{:S(2)}) copy-start(f32[32768]{0:T(1024)} %param.10) | copy-start | bytes 393220
  3.5 0.9 %copy-start.2 = (f32[32768]{0:T(1024)S(1)}, f32[32768]{0:T(1024)}, u32[]{:S(2)}) copy-start(f32[32768]{0:T(1024)} %param.11) | copy-start | bytes 393220
  4.4 0.9 %copy-start.3 = (f32[32768]{0:T(1024)S(1)}, f32[32768]{0:T(1024)}, u32[]{:S(2)}) copy-start(f32[32768]{0:T(1024)} %param.12) | copy-start | bytes 393220
  5.3 0.9 %copy-start.4 = (s32[32768]{0:T(1024)S(1)}, s32[32768]{0:T(1024)}, u32[]{:S(2)}) copy-start(s32[32768]{0:T(1024)} %param.15) | copy-start | bytes 393220

commit v2 on v1

--- a/solution.py
+++ b/solution.py
@@ -22,7 +22,7 @@
     PAIR_AT[(_j, _i)] = _n
 BAND_ROWS = 48
 USED_ROWS = 44
-STEP = 512
+STEP = 4096
 HI = 256
 LO = SRC_DEV // HI
 
@@ -49,16 +49,24 @@
     n_src,
     n_att,
     att_ref,
+    val_hbm,
+    wgt_hbm,
+    time_hbm,
+    apart_hbm,
+    spart_hbm,
+    ids_hbm,
+    knot_ref,
+    valid_ref,
+    step_ref,
+    out_ref,
     val_ref,
     wgt_ref,
     time_ref,
     apart_ref,
     spart_ref,
     ids_ref,
-    knot_ref,
-    valid_ref,
-    step_ref,
-    out_ref,
+    in_sem,
+    mixed,
     vt,
     pt,
     bt,
@@ -95,9 +103,24 @@
     me = lax.axis_index("src")
     seg = lax.axis_index("att")
     per = part.shape[1]
-    nblock, width = val_ref.shape
+    nblock, width = val_hbm.shape
     count = att_ref.shape[1]
     barrier = pltpu.get_barrier_semaphore()
+    loads = [
+        pltpu.make_async_copy(source, place, in_sem.at[n])
+        for n, (source, place) in enumerate(
+            [
+                (apart_hbm, apart_ref),
+                (wgt_hbm, wgt_ref),
+                (time_hbm, time_ref),
+                (val_hbm, val_ref),
+                (spart_hbm, spart_ref),
+                (ids_hbm, ids_ref),
+            ]
+        )
+    ]
+    for load in loads:
+        load.start()
 
     def greet(t, carry):
         pl.semaphore_signal(
@@ -119,6 +142,20 @@
 
         lax.fori_loop(0, n_src, greet_across, 0)
 
+    loads[0].wait()
+
+    def mix(g, carry):
+        for t in range(8):
+            at = pl.multiple_of((g * 8 + t) * 2 * width, 2 * width)
+            both = apart_ref[:, pl.ds(at, 2 * width)]
+            mixed[pl.ds(pl.multiple_of((g * 8 + t) * 8, 8), 8), :] = jnp.concatenate(
+                [both[:, :width], both[:, width:]], axis=0
+            )
+        return carry
+
+    lax.fori_loop(0, nblock // 16, mix, 0)
+    for load in loads[1:4]:
+        load.wait()
     position = lax.broadcasted_iota(jnp.int32, (width, nblock), 0)
     weight = jnp.where(position < valid_ref[...], wgt_ref[...].T, 0.0)
     wr[...] = weight.T
@@ -128,7 +165,7 @@
     basis = basis_of(time_ref[...].T)
     for j in range(4):
         bt[j] = basis[j]
-        pt[j] = apart_ref[j].T
+        pt[j] = mixed[pl.ds(j, nblock, stride=4), :].T
     wvalue = weight * value
     for n, (i, j) in enumerate(PAIRS):
         wpp[n] = weight * pt[i] * pt[j]
@@ -267,6 +304,8 @@
 
     steps = nblock * width // STEP
     acc_s[...] = jnp.zeros_like(acc_s)
+    loads[4].wait()
+    loads[5].wait()
     lax.fori_loop(0, steps // 2, s_step, 0)
 
     lax.fori_loop(1, n_src, finish(rs_wait), 0)
@@ -557,6 +596,7 @@
         f32 = jnp.float32
         dma = pltpu.SemaphoreType.DMA
         vmem = pl.BlockSpec(memory_space=pltpu.VMEM)
+        hbm = pl.BlockSpec(memory_space=pltpu.HBM)
         tall = (width, nblock)
         return pl.pallas_call(
             functools.partial(kernel, n_src, n_att),
@@ -564,9 +604,17 @@
                 jax.ShapeDtypeStruct((4, count), f32),
                 jax.ShapeDtypeStruct((5, SRC_DEV), f32),
             ),
-            in_specs=[vmem] * 9,
+            in_specs=[vmem] + [hbm] * 6 + [vmem] * 2,
             out_specs=(vmem, vmem),
             scratch_shapes=[
+                pltpu.VMEM((nblock, width), f32),
+                pltpu.VMEM((nblock, width), f32),
+                pltpu.VMEM((nblock, width), f32),
+                pltpu.VMEM((4, nblock * width), f32),
+                pltpu.VMEM((5, nblock * width), f32),
+                pltpu.VMEM((nblock, width), jnp.int32),
+                dma((6,)),
+                pltpu.VMEM((4 * nblock, width), f32),
                 pltpu.VMEM((2,) + tall, f32),
                 pltpu.VMEM((4,) + tall, f32),
                 pltpu.VMEM((4,) + tall, f32),
@@ -610,7 +658,7 @@
             obs_value.reshape(nblock, width),
             obs_weight.reshape(nblock, width),
             obs_time.reshape(nblock, width),
-            att_partials.reshape(4, nblock, width),
+            att_partials,
             src_partials,
             obs_source.reshape(nblock, width),
             knot_start.reshape(1, nblock),

time: 60.9 us -> 39.9 us (0.66)
  Pallas kernels: 53.2 us -> 31.1 us
  local copies, waits for them, and re-layouts: 6.75 us -> 7.82 us
    pallas_call x1, Pallas kernels: 53.2 us -> 31.1 us  [shards(): pl.pallas_call(functools.partial(kernel, n_src, n_att), out_shape=(jax.Sh...]
    unnamed x19 -> x20, local copies, waits for them, and re-layouts: 6.75 us -> 7.82 us
where the time goes in v2:
time: 39.9 us; the launch traced here: 39.6 us
  Pallas kernels  31.1 us (78%)
  local copies, waits for them, and re-layouts  7.82 us (20%)
  between operations  0.67 us (2%)
    pallas_call x1, Pallas kernels, shards(): pl.pallas_call(functools.partial(kernel, n_src, n_att), out_shape=(jax.Sh...  31.1 us
    unnamed x20, local copies, waits for them, and re-layouts  7.82 us

profile of v2, /device:TPU:0, one launch (start us, length us, event | category | flops | bytes accessed | tf_op | source)
XLA Modules:
  0.0 39.6 jit_solution(9275352193666815022)
XLA Ops:
  0.6 0.0 copy-start.6
  0.6 0.0 copy-start.8
  0.7 0.0 copy-start.7
  0.7 0.7 %copy-done.6 = f32[4,256]{1,0:T(4,128)S(1)} copy-done((f32[4,256]{1,0:T(4,128)S(1)}, f32[4,256]{1,0:T(4,128)}, u32[]{:S(2)}) %copy-start.6) | copy-done | bytes 4120
  1.3 0.0 copy-done.8
  1.3 0.0 copy-done.7
  1.3 0.0 copy-start
  1.3 1.2 %copy-done = f32[5,32768]{1,0:T(8,128)S(1)} copy-done((f32[5,32768]{1,0:T(8,128)S(1)}, f32[5,32768]{1,0:T(8,128)}, u32[]{:S(2)}) %copy-start) | copy-done | bytes 655384
  2.6 0.0 copy-start.1
  2.6 1.0 %copy-done.1 = f32[4,32768]{1,0:T(4,128)S(1)} copy-done((f32[4,32768]{1,0:T(4,128)S(1)}, f32[4,32768]{1,0:T(4,128)}, u32[]{:S(2)}) %copy-start.1) | copy-done | bytes 524312
  3.6 0.0 copy-start.2
  3.6 0.9 %copy-done.2 = f32[32768]{0:T(1024)S(1)} copy-done((f32[32768]{0:T(1024)S(1)}, f32[32768]{0:T(1024)}, u32[]{:S(2)}) %copy-start.2) | copy-done | bytes 131096
  4.5 0.0 copy-start.3
  4.5 0.9 %copy-done.3 = f32[32768]{0:T(1024)S(1)} copy-done((f32[32768]{0:T(1024)S(1)}, f32[32768]{0:T(1024)}, u32[]{:S(2)}) %copy-start.3) | copy-done | bytes 131096
  5.4 0.0 copy-start.4
  5.4 0.9 %copy-done.4 = f32[32768]{0:T(1024)S(1)} copy-done((f32[32768]{0:T(1024)S(1)}, f32[32768]{0:T(1024)}, u32[]{:S(2)}) %copy-start.4) | copy-done | bytes 131096
  6.3 0.0 copy-start.5
  6.3 0.9 %copy-done.5 = s32[32768]{0:T(1024)S(1)} copy-done((s32[32768]{0:T(1024)S(1)}, s32[32768]{0:T(1024)}, u32[]{:S(2)}) %copy-start.5) | copy-done | bytes 131096
  7.2 31.1 %shard_map.104 = (f32[4,256]{1,0:T(4,128)S(1)}, f32[5,4096]{1,0:T(8,128)S(1)}) custom-call(f32[4,256]{1,0:T(4,128)S(1)} %copy-done.6, f32[256,128]{1,0:T(8,128)S(1)} %bitcast.6, f32[256,128]{1,0:T(8,128)S(1)} %bitcast.7, f32[256,128]{1,0:T(8,128)S(1)} %bitcast.8, f32[4,32768]{1,0:T(4,128)S(1)} %copy-done.1, f32[5,32768]{1,0:T(8,128)S(1)} %copy-done, ...), custom_call_target="tpu_custom_call" | custom-call | tf_op jit(solution)/shard_map/pallas_call | solution.py:601
  38.3 0.6 %copy.13 = f32[4,256]{1,0:T(4,128)} copy(f32[4,256]{1,0:T(4,128)S(1)} %get-tuple-element.4) | data formatting | bytes 8192
  38.9 0.7 %copy.14 = f32[5,4096]{1,0:T(8,128)} copy(f32[5,4096]{1,0:T(8,128)S(1)} %get-tuple-element.5) | data formatting | bytes 163840
Async XLA Ops:
  0.6 0.7 %copy-start.6 = (f32[4,256]{1,0:T(4,128)S(1)}, f32[4,256]{1,0:T(4,128)}, u32[]{:S(2)}) copy-start(f32[4,256]{1,0:T(4,128)} %att_ref.1) | copy-start | bytes 12292
  0.6 0.7 %copy-start.8 = (s32[256]{0:T(256)S(1)}, s32[256]{0:T(256)}, u32[]{:S(2)}) copy-start(s32[256]{0:T(256)} %param.17) | copy-start | bytes 3076
  0.7 0.7 %copy-start.7 = (s32[256]{0:T(256)S(1)}, s32[256]{0:T(256)}, u32[]{:S(2)}) copy-start(s32[256]{0:T(256)} %param.16) | copy-start | bytes 3076
  1.3 1.2 %copy-start = (f32[5,32768]{1,0:T(8,128)S(1)}, f32[5,32768]{1,0:T(8,128)}, u32[]{:S(2)}) copy-start(f32[5,32768]{1,0:T(8,128)} %spart_hbm.1) | copy-start | bytes 1966084
  2.6 1.0 %copy-start.1 = (f32[4,32768]{1,0:T(4,128)S(1)}, f32[4,32768]{1,0:T(4,128)}, u32[]{:S(2)}) copy-start(f32[4,32768]{1,0:T(4,128)} %apart_hbm.1) | copy-start | bytes 1572868
  3.6 0.9 %copy-start.2 = (f32[32768]{0:T(1024)S(1)}, f32[32768]{0:T(1024)}, u32[]{:S(2)}) copy-start(f32[32768]{0:T(1024)} %param.10) | copy-start | bytes 393220
  4.5 0.9 %copy-start.3 = (f32[32768]{0:T(1024)S(1)}, f32[32768]{0:T(1024)}, u32[]{:S(2)}) copy-start(f32[32768]{0:T(1024)} %param.11) | copy-start | bytes 393220
  5.4 0.9 %copy-start.4 = (f32[32768]{0:T(1024)S(1)}, f32[32768]{0:T(1024)}, u32[]{:S(2)}) copy-start(f32[32768]{0:T(1024)} %param.12) | copy-start | bytes 393220
  6.3 0.9 %copy-start.5 = (s32[32768]{0:T(1024)S(1)}, s32[32768]{0:T(1024)}, u32[]{:S(2)}) copy-start(s32[32768]{0:T(1024)} %param.15) | copy-start | bytes 393220

commit v3 on v2

--- a/solution.py
+++ b/solution.py
@@ -22,6 +22,7 @@
     PAIR_AT[(_j, _i)] = _n
 BAND_ROWS = 48
 USED_ROWS = 44
+GIVE_AFTER = 3
 STEP = 4096
 HI = 256
 LO = SRC_DEV // HI
@@ -306,14 +307,6 @@
     acc_s[...] = jnp.zeros_like(acc_s)
     loads[4].wait()
     loads[5].wait()
-    lax.fori_loop(0, steps // 2, s_step, 0)
-
-    lax.fori_loop(1, n_src, finish(rs_wait), 0)
-    total = slots[0]
-    for s in range(1, n_src):
-        total = total + slots[s]
-    full[me] = total
-
     def ag_copy(t):
         c = lax.rem(me + t, n_src)
         return pltpu.make_async_remote_copy(
@@ -356,17 +349,30 @@
             device_id_type=MESH,
         )
 
-    lax.fori_loop(1, n_src, run(ag_copy), 0)
-
-    @pl.when(seg < n_att - 1)
-    def _():
-        lax.fori_loop(0, n_src, run(lambda t: right_copy(lax.rem(me + t, n_src), me)), 0)
-
-    @pl.when(seg > 0)
-    def _():
-        lax.fori_loop(0, n_src, run(lambda t: left_copy(lax.rem(me + t, n_src), me)), 0)
-
-    lax.fori_loop(steps // 2, steps, s_step, 0)
+    def give():
+        lax.fori_loop(1, n_src, finish(rs_wait), 0)
+        total = slots[0]
+        for s in range(1, n_src):
+            total = total + slots[s]
+        full[me] = total
+
+        lax.fori_loop(1, n_src, run(ag_copy), 0)
+
+        @pl.when(seg < n_att - 1)
+        def _():
+            lax.fori_loop(0, n_src, run(lambda t: right_copy(lax.rem(me + t, n_src), me)), 0)
+
+        @pl.when(seg > 0)
+        def _():
+            lax.fori_loop(0, n_src, run(lambda t: left_copy(lax.rem(me + t, n_src), me)), 0)
+
+
+    def s_and_give(g, carry):
+        s_step(g, carry)
+        pl.when(g == GIVE_AFTER)(give)
+        return carry
+
+    lax.fori_loop(0, steps, s_and_give, 0)
 
     def mine(buf, c, half):
         return buf[c, :, half * 128 : half * 128 + 128]
@@ -651,7 +657,7 @@
             compiler_params=pltpu.CompilerParams(
                 collective_id=0,
                 has_side_effects=True,
-                vmem_limit_bytes=48 * 1024 * 1024,
+                vmem_limit_bytes=56 * 1024 * 1024,
             ),
         )(
             attitude,

time: 39.9 us -> 35.6 us (0.89)
  local copies, waits for them, and re-layouts: 7.82 us -> 2.85 us
  Pallas kernels: 31.1 us -> 31.8 us
    unnamed x20 -> x2, local copies, waits for them, and re-layouts: 7.82 us -> 2.85 us
    pallas_call x1, Pallas kernels: 31.1 us -> 31.8 us  [shards(): pl.pallas_call(functools.partial(kernel, n_src, n_att), out_shape=(jax.Sh...]
where the time goes in v3:
time: 35.6 us; the launch traced here: 35.3 us
  Pallas kernels  31.8 us (89%)
  local copies, waits for them, and re-layouts  2.85 us (8%)
  between operations  0.64 us (2%)
    pallas_call x1, Pallas kernels, shards(): pl.pallas_call(functools.partial(kernel, n_src, n_att), out_shape=(jax.Sh...  31.8 us
    unnamed x2, local copies, waits for them, and re-layouts  2.85 us

profile of v3, /device:TPU:0, one launch (start us, length us, event | category | flops | bytes accessed | tf_op | source)
XLA Modules:
  0.0 35.3 jit_solution(8025825852699742837)
XLA Ops:
  0.6 31.8 %shard_map.104 = (f32[4,256]{1,0:T(4,128)}, f32[5,4096]{1,0:T(8,128)}) custom-call(f32[4,256]{1,0:T(4,128)} %att_ref.1, f32[256,128]{1,0:T(8,128)} %bitcast.6, f32[256,128]{1,0:T(8,128)} %bitcast.7, f32[256,128]{1,0:T(8,128)} %bitcast.8, f32[4,32768]{1,0:T(4,128)} %apart_hbm.1, f32[5,32768]{1,0:T(8,128)} %spart_hbm.1, s32[256,128]{1,0:T(8,128)} %bitcast.9, ...), custom_call_target="tpu_custom_call" | custom-call | tf_op jit(solution)/shard_map/pallas_call | solution.py:607
  32.5 1.3 %copy.13 = f32[4,256]{1,0:T(4,128)} copy(f32[4,256]{1,0:T(4,128)} %get-tuple-element.4) | data formatting | bytes 8192
  33.8 1.6 %copy.14 = f32[5,4096]{1,0:T(8,128)} copy(f32[5,4096]{1,0:T(8,128)} %get-tuple-element.5) | data formatting | bytes 163840
